TPU v7x, 256 devices: a whole 4x4x8 slice. The times are simulated.
256 devices in a mesh: blk: 64 (over y, x, z_hi), grp: 4 (over z_lo, core).
Axes of the slice: x: 4, y: 4, z: 8 (z_hi: 4, z_lo: 2; z = z_hi * 2 + z_lo), core: 2. Of those that a mesh axis runs over, the one named last changes fastest.
Arguments:
- embeddings: bfloat16 [131072, 1024], P(('blk', 'grp')), may hold values from -1 to 1, as said below
- partners: int32 [3, 64], replicated, may hold values from 0 to 63, as said below
Outputs:
- density: float32 [131072], P(('blk', 'grp'))
Inputs may be any that keep to these rules, and one draw needn't show every extreme that they name: Each row of partners pairs the 64 groups: partners[r, partners[r, g]] = g and partners[r, g] != g; no two rounds pair the same two groups. `embeddings`: every row has squared norm 1 up to bfloat16 rounding.
All inputs are finite; a program needn't handle non-finite values.
Results may differ from a plain program's by a relative error of at most 0.0003.
Values may be sent and summed in bfloat16 or wider, within the bound.
A program may use at most 64 MiB of HBM per device.

v0:
```python
import jax
import jax.numpy as jnp
from jax import lax
from jax.sharding import PartitionSpec as P

SOFTMAX_HEAT = 0.05


def scorer(members, columns):
    score_values = lax.dot_general(
        members, columns, (((1,), (1,)), ((), ())), preferred_element_type=jnp.float32
    )
    return jnp.exp((score_values - 1.0) / SOFTMAX_HEAT)


def body(embeddings, partners):
    row_count = embeddings.shape[0]
    feat_width = embeddings.shape[1]
    block_list = lax.axis_size("blk")
    member = lax.axis_index("grp")
    rounds = partners.shape[0]
    row_index = member * row_count + jnp.arange(row_count, dtype=jnp.int32)
    spread = lax.all_to_all(
        embeddings.reshape(block_list, row_count // block_list, feat_width),
        "blk",
        split_axis=0,
        concat_axis=0,
        tiled=True,
    )
    routed = []
    for turn_index in range(rounds):
        outgoing = jnp.take(spread, partners[turn_index], axis=0)
        arrived = lax.all_to_all(outgoing, "blk", split_axis=0, concat_axis=0, tiled=True)
        routed.append(arrived.reshape(row_count, feat_width))
    segment = lax.all_gather(embeddings, "grp", axis=0, tiled=True)
    col_index = jnp.arange(segment.shape[0], dtype=jnp.int32)
    own_terms = jnp.where(
        row_index[:, None] == col_index[None, :], jnp.float32(0.0), scorer(embeddings, segment)
    )
    density = jnp.sum(own_terms, axis=1)
    for turn_index in range(rounds):
        density = density + jnp.sum(
            scorer(embeddings, lax.all_gather(routed[turn_index], "grp", axis=0, tiled=True)),
            axis=1,
        )
    return density


def solution(mesh):
    return jax.shard_map(
        body,
        mesh=mesh,
        in_specs=(P(("blk", "grp"), None), P()),
        out_specs=P(("blk", "grp")),
        check_vma=False,
    )
```

profile of v0, /device:TPU:8, one launch (start us, length us, event | category | flops | bytes accessed | tf_op | source)
XLA Modules:
  0.0 307.4 jit_solution(10366431394410392302)
XLA Ops:
  6.5 0.0 all-gather.5.cloned.1.call-start
  6.5 0.7 all-gather.5.cloned.1.call-update
  7.3 14.6 %all-to-all-start = ((bf16[64,8,1024]{2,1,0:T(8,128)(2,1)}), bf16[64,8,1024]{2,1,0:T(8,128)(2,1)S(1)}, u32[]{:S(2)}, u32[]{:S(2)}) async-start(bf16[64,8,1024]{2,1,0:T(8,128)(2,1)} %bitcast.21), calls=%async_computation | async-start | bytes 2097152 | tf_op jit(solution)/shard_map/all_to_all | solution.py:23
  21.8 0.0 all-gather.9.cloned.1.call-start
  21.9 0.8 compare_and_fusion.2
  22.7 38.7 %all-to-all-done = bf16[64,8,1024]{2,1,0:T(8,128)(2,1)S(1)} async-done(((bf16[64,8,1024]{2,1,0:T(8,128)(2,1)}), bf16[64,8,1024]{2,1,0:T(8,128)(2,1)S(1)}, u32[]{:S(2)}, u32[]{:S(2)}) %all-to-all-start) | async-done | bytes 1048608 | tf_op jit(solution)/shard_map/all_to_all | solution.py:23
  61.4 0.6 gather_fusion.1
  62.0 0.2 broadcast_select_fusion.1
  62.2 45.8 %all_to_all.20 = bf16[64,8,1024]{2,1,0:T(8,128)(2,1)} all-to-all(bf16[64,8,1024]{2,1,0:T(8,128)(2,1)S(1)} %broadcast_select_fusion.1), channel_id=1, replica_groups=mesh['blk'=64,'grp'=4] {'blk'}, dimensions={0} | all-to-all | bytes 2097152 | tf_op jit(solution)/shard_map/all_to_all | solution.py:33
  108.0 0.0 all-gather.9.cloned.1.call-update
  108.0 0.0 all-gather.7.cloned.1.call-start
  108.1 0.6 gather_fusion
  108.7 0.2 broadcast_select_fusion.2
  108.9 44.8 %all_to_all.21 = bf16[64,8,1024]{2,1,0:T(8,128)(2,1)} all-to-all(bf16[64,8,1024]{2,1,0:T(8,128)(2,1)S(1)} %broadcast_select_fusion.2), channel_id=1, replica_groups=mesh['blk'=64,'grp'=4] {'blk'}, dimensions={0} | all-to-all | bytes 2097152 | tf_op jit(solution)/shard_map/all_to_all | solution.py:33
  153.7 0.0 copy-start
  153.7 0.0 all-gather.7.cloned.1.call-update
  153.7 0.0 all-gather.11.cloned.1.call-start
  153.8 0.6 gather_fusion.2
  154.4 0.2 broadcast_select_fusion
  154.6 44.7 %all_to_all.22 = bf16[64,8,1024]{2,1,0:T(8,128)(2,1)} all-to-all(bf16[64,8,1024]{2,1,0:T(8,128)(2,1)S(1)} %broadcast_select_fusion), channel_id=1, replica_groups=mesh['blk'=64,'grp'=4] {'blk'}, dimensions={0} | all-to-all | bytes 2097152 | tf_op jit(solution)/shard_map/all_to_all | solution.py:33
  199.3 0.0 all-gather.11.cloned.1.call-update
  199.4 0.0 all-gather.5.cloned.1.call-done
  199.4 0.0 copy-done
  199.4 5.1 %select_reduce_fusion = f32[512]{0:T(512)S(1)} fusion(bf16[512,1024]{1,0:T(8,128)(2,1)S(1)} %copy-done, bf16[2048,1024]{1,0:T(8,128)(2,1)} %all-gather.5.cloned.1.call-done, s32[512]{0:T(512)S(1)} %iota_add_fusion), kind=kOutput, calls=%fused_computation.6 | convolution fusion | flops 2152726016 | bytes 5246976 | tf_op jit(solution)/shard_map/dot_general | solution.py:10
  204.5 0.0 all-gather.9.cloned.1.call-done
  204.5 4.9 %exponential_reduce_fusion.1 = f32[512]{0:T(512)S(1)} fusion(bf16[2048,1024]{1,0:T(8,128)(2,1)} %all-gather.9.cloned.1.call-done, bf16[512,1024]{1,0:T(8,128)(2,1)S(1)} %copy-done), kind=kOutput, calls=%fused_computation.4 | convolution fusion | flops 2150628864 | bytes 5244928 | tf_op jit(solution)/shard_map/dot_general | solution.py:10
  209.4 34.8 %all-gather.7.cloned.1.call-done = bf16[2048,1024]{1,0:T(8,128)(2,1)} async-done(((bf16[512,1024]{1,0:T(8,128)(2,1)}), bf16[2048,1024]{1,0:T(8,128)(2,1)}) %all-gather.7.cloned.1.call-update) | async-done | bytes 4194320 | tf_op jit(solution)/shard_map/all_gather | solution.py:43
  244.2 5.0 %exponential_reduce_fusion.2 = f32[512]{0:T(512)S(1)} fusion(bf16[2048,1024]{1,0:T(8,128)(2,1)} %all-gather.7.cloned.1.call-done, bf16[512,1024]{1,0:T(8,128)(2,1)S(1)} %copy-done), kind=kOutput, calls=%fused_computation.5 | convolution fusion | flops 2150628864 | bytes 5244928 | tf_op jit(solution)/shard_map/dot_general | solution.py:10
  249.1 46.2 %all-gather.11.cloned.1.call-done = bf16[2048,1024]{1,0:T(8,128)(2,1)} async-done(((bf16[512,1024]{1,0:T(8,128)(2,1)}), bf16[2048,1024]{1,0:T(8,128)(2,1)}) %all-gather.11.cloned.1.call-update) | async-done | bytes 4194320 | tf_op jit(solution)/shard_map/all_gather | solution.py:43
  295.3 4.9 %exponential_reduce_fusion = f32[512]{0:T(512)S(1)} fusion(bf16[2048,1024]{1,0:T(8,128)(2,1)} %all-gather.11.cloned.1.call-done, bf16[512,1024]{1,0:T(8,128)(2,1)S(1)} %copy-done), kind=kOutput, calls=%fused_computation.3 | convolution fusion | flops 2150628864 | bytes 5244928 | tf_op jit(solution)/shard_map/dot_general | solution.py:10
  300.3 0.6 add_add_fusion
  (4 shorter events, 0.0 us)
Async XLA Ops:
  6.5 192.8 %all-gather.5.cloned.1.call-start = ((), (), s32[]{:S(2)}) async-start(), calls=%async_computation.4 | async-start | bytes 5242880 | tf_op jit(solution)/shard_map/all_gather | solution.py:35
  7.3 54.1 %all-to-all-start = ((bf16[64,8,1024]{2,1,0:T(8,128)(2,1)}), bf16[64,8,1024]{2,1,0:T(8,128)(2,1)S(1)}, u32[]{:S(2)}, u32[]{:S(2)}) async-start(bf16[64,8,1024]{2,1,0:T(8,128)(2,1)} %bitcast.21), calls=%async_computation | async-start | bytes 2097152 | tf_op jit(solution)/shard_map/all_to_all | solution.py:23
  21.8 182.6 %all-gather.9.cloned.1.call-start = ((), (), s32[]{:S(2)}) async-start(), calls=%async_computation.6 | async-start | bytes 5242880 | tf_op jit(solution)/shard_map/all_gather | solution.py:43
  108.0 136.1 %all-gather.7.cloned.1.call-start = ((), (), s32[]{:S(2)}) async-start(), calls=%async_computation.5 | async-start | bytes 5242880 | tf_op jit(solution)/shard_map/all_gather | solution.py:43
  153.7 45.7 %copy-start = (bf16[512,1024]{1,0:T(8,128)(2,1)S(1)}, bf16[512,1024]{1,0:T(8,128)(2,1)}, u32[]{:S(2)}) copy-start(bf16[512,1024]{1,0:T(8,128)(2,1)} %param.4) | copy-start | bytes 3145732
  153.7 141.6 %all-gather.11.cloned.1.call-start = ((), (), s32[]{:S(2)}) async-start(), calls=%async_computation.7 | async-start | bytes 5242880 | tf_op jit(solution)/shard_map/all_gather | solution.py:43
Sparse Core Ops, SparseCore 0:
  9.2 92.1 all-gather.4
  108.2 85.3 all-gather.8
  195.4 48.7 all-gather.6
  245.8 49.4 all-gather.10
where the time goes:
time: 310 us; the launch traced here: 307 us
  blocking collectives  135 us (44%)
  waiting for transfers between devices  120 us (39%)
  matrix products  19.9 us (6%)
  starting transfers between devices  14.7 us (5%)
  between operations  13.3 us (4%)
    all_to_all x3, blocking collectives, body(): lax.all_to_all(outgoing, 'blk', split_axis=0, concat_axis=0, tiled=True)  135 us
    all_gather x3, waiting for transfers between devices, body(): lax.all_gather(routed[turn_index], 'grp', axis=0, tiled=True)  81 us
    all_to_all x1, waiting for transfers between devices, body(): lax.all_to_all(embeddings.reshape(block_list, row_count // block_list, fe...  38.7 us
    dot_general x4, matrix products, scorer(): lax.dot_general(members, columns, (((1,), (1,)), ((), ())), preferred_ele...  19.9 us
    all_to_all x1, starting transfers between devices, body(): lax.all_to_all(embeddings.reshape(block_list, row_count // block_list, fe...  14.6 us
  transfers between devices with their start and end apart: 5, of which 3 were waited for; matrix products, arithmetic and copies ran while one was open for 6% of the time, Pallas kernels for 0%

commit v1 on v0

v1 whole, which is shorter than its diff:
```python
import math

import jax
import jax.numpy as jnp
from jax import lax
from jax.experimental import pallas as pl
from jax.experimental.pallas import tpu as pltpu
from jax.sharding import PartitionSpec as P

MESH = pl.DeviceIdType.MESH
HEAT = 0.05
RATE = math.log2(math.e) / HEAT
GROUPS = 64
ROWS = 512
WIDTH = 1024
TILE = 256


def similarity(columns, members):
    c = lax.dot_general(columns, members, (((1,), (1,)), ((), ())), preferred_element_type=jnp.float32)
    return jnp.exp2(c * RATE - RATE)


def lane_sums(total):
    ones = jnp.ones((8, 128), jnp.float32)
    return lax.dot_general(
        ones, total, (((1,), (1,)), ((), ())),
        precision=lax.Precision.HIGHEST, preferred_element_type=jnp.float32,
    )


def kernel(
    partners, x, out,
    own, pieces, stage1, stage2, met1, met2, own_acc, acc1, acc2, row_acc, row_in, col_out, col_all,
    hop_a, low_a, hop_b, low_b, pick1, pick2,
    line_y, line_z, other, spread_send, spread_recv, send1, recv1, send2, recv2,
    own_send, own_recv, fwd_send, fwd_recv, row_send, row_recv, col_send, col_recv,
):
    blk, grp = lax.axis_index("blk"), lax.axis_index("grp")
    y, xx, h = blk // 16, (blk // 4) % 4, blk % 4
    e, c = grp // 2, grp % 2

    def at(y_, x_, h_, e_=None, c_=None):
        e_ = e if e_ is None else e_
        c_ = c if c_ is None else c_
        return ((y_ % 4) * 16 + (x_ % 4) * 4 + h_ % 4, e_ * 2 + c_)

    def signal(sem, device):
        pl.semaphore_signal(sem, inc=1, device_id=device, device_id_type=MESH)

    def remote(src, dst, send, recv, device):
        return pltpu.make_async_remote_copy(
            src_ref=src, dst_ref=dst, send_sem=send, recv_sem=recv, device_id=device, device_id_type=MESH
        )

    def drain(ref, sem):
        pltpu.make_async_copy(ref, ref, sem).wait()

    barrier = pltpu.get_barrier_semaphore()
    for i in (1, 2, 3):
        signal(barrier, at(y + i, xx, h))
        signal(barrier, at(y, xx + i, h))
        signal(barrier, at(y, xx, h + i))
    signal(barrier, at(y, xx, h, 1 - e))
    signal(barrier, at(y, xx, h, e, 1 - c))
    signal(barrier, at(y, xx, h, 1 - e, 1 - c))
    pl.semaphore_wait(barrier, 12)
    own_core = remote(x, own.at[grp], own_send.at[0], own_recv.at[0], at(y, xx, h, e, 1 - c))
    own_core.start()
    for i in (1, 2, 3):
        signal(line_y, at(y + i, xx, h))
    pl.semaphore_wait(line_y, 3)
    for i in (1, 2, 3):
        signal(line_z, at(y, xx, h + i))
    pl.semaphore_wait(line_z, 3)

    def spread(k, carry):
        ty, tx, th = (y + k // 16) % 4, (xx + (k // 4) % 4) % 4, (h + k) % 4
        row = pl.multiple_of((th * 8 + ty * 2 + tx // 2) * 16, 16)
        col = pl.multiple_of((tx % 2) * 512, 512)
        remote(
            x.at[pl.ds(row, 16), pl.ds(col, 512)], pieces.at[blk], spread_send, spread_recv, at(ty, tx, th)
        ).start()
        return carry

    lax.fori_loop(1, GROUPS, spread, 0)
    my_row = pl.multiple_of((h * 8 + y * 2 + xx // 2) * 16, 16)
    my_col = pl.multiple_of((xx % 2) * 512, 512)
    pieces[blk] = x[pl.ds(my_row, 16), pl.ds(my_col, 512)]

    def mate(g):
        return g + 4 - 8 * ((g // 4) % 2)

    def begin(g, carry):
        hop_a[0, g] = partners[1, partners[0, g]]
        hop_b[0, g] = mate(partners[2, g])
        low_a[g] = g
        low_b[g] = g
        return carry

    lax.fori_loop(0, GROUPS, begin, 0)
    for step in range(5):
        now, later = step % 2, (step + 1) % 2

        def double(g, carry):
            s, t = hop_a[now, g], hop_b[now, g]
            low_a[g] = jnp.minimum(low_a[g], low_a[s])
            low_b[g] = jnp.minimum(low_b[g], low_b[t])
            hop_a[later, g] = hop_a[now, s]
            hop_b[later, g] = hop_b[now, t]
            return carry

        lax.fori_loop(0, GROUPS, double, 0)

    def first(g):
        return low_a[g] < low_a[partners[0, g]]

    def receives(g):
        return low_b[g] < low_b[partners[2, g]]

    def choose(g, carry):
        pick1[g] = jnp.where(first(g), partners[0, g], partners[1, g])
        pick2[g] = partners[2, jnp.where(receives(g), g, mate(g))]
        return carry

    lax.fori_loop(0, GROUPS, choose, 0)

    own_acc[...] = jnp.zeros_like(own_acc)
    diagonal = lax.broadcasted_iota(jnp.int32, (ROWS, TILE), 0)
    across = lax.broadcasted_iota(jnp.int32, (ROWS, TILE), 1)

    def own_tile(t, carry):
        start = pl.multiple_of(t * TILE, TILE)
        block = x[pl.ds(start, TILE), :]
        own[grp, pl.ds(start, TILE), :] = block
        terms = jnp.where(diagonal == across + t * TILE, 0.0, similarity(x[...], block))
        own_acc[...] += terms[:, :128] + terms[:, 128:]
        return carry

    lax.fori_loop(0, ROWS // TILE, own_tile, 0)

    def own_others(member):
        def tile(t, carry):
            terms = similarity(x[...], own[member, pl.ds(pl.multiple_of(t * TILE, TILE), TILE), :])
            own_acc[...] += terms[:, :128] + terms[:, 128:]
            return carry

        lax.fori_loop(0, ROWS // TILE, tile, 0)

    own_core.wait()
    own_others(e * 2 + 1 - c)

    drain(pieces.at[pl.ds(0, GROUPS - 1)], spread_recv)
    signal(other, at(y, xx, h, 1 - e))
    pl.semaphore_wait(other, 1)
    own_chip = remote(x, own.at[grp], own_send.at[1], own_recv.at[1], at(y, xx, h, 1 - e))
    own_chip.start()

    def place(k):
        d = k % 4
        ty, tx, th = (y + k // 16) % 4, (xx + (k // 4) % 4) % 4, (h + k) % 4
        to = jnp.where(d == 0, e, jnp.where(d == 1, 0, jnp.where(d == 3, 1, 1 - e)))
        second0 = jnp.where(e == 0, d, d - 1)
        second1 = jnp.where(e == 0, 3 - d, jnp.where(d == 0, 0, 1))
        slot = 2 * e + jnp.where(to == 0, second0, second1)
        row = pl.multiple_of(slot * 128 + (y * 2 + xx // 2) * 16, 16)
        return ty, tx, th, to, row

    def half_units(k, carry):
        ty, tx, th, to, row = place(k)
        lane = pl.multiple_of((tx % 2) * 256, 256)
        stage2[k] = pieces[pick2[ty * 16 + tx * 4 + th], :, pl.ds(lane, 256)]
        col = pl.multiple_of((xx % 2) * 512 + (tx % 2) * 256, 256)
        remote(
            stage2.at[k], met2.at[pl.ds(row, 16), pl.ds(col, 256)], send2, recv2, at(ty, tx, th, to)
        ).start()
        return carry

    def units(k, carry):
        ty, tx, th, to, row = place(k)
        stage1[k] = pieces[pick1[ty * 16 + tx * 4 + th]]
        remote(
            stage1.at[k], met1.at[pl.ds(row, 16), pl.ds(my_col, 512)], send1, recv1, at(ty, tx, th, to)
        ).start()
        return carry

    lax.fori_loop(1, GROUPS, half_units, 0)
    lax.fori_loop(1, GROUPS, units, 0)
    home = pl.multiple_of((2 * e + 0) * 128 + (y * 2 + xx // 2) * 16, 16)
    half = pl.multiple_of((xx % 2) * 256, 256)
    met1[pl.ds(home, 16), pl.ds(my_col, 512)] = pieces[pick1[blk]]
    met2[pl.ds(home, 16), pl.ds(pl.multiple_of(my_col + half, 256), 256)] = pieces[
        pick2[blk], :, pl.ds(half, 256)
    ]

    own_chip.wait()
    across_core = remote(
        own.at[2 - 2 * e + c], own.at[2 - 2 * e + c], own_send.at[2], own_recv.at[2], at(y, xx, h, e, 1 - c)
    )
    across_core.start()
    own_others(2 - 2 * e + c)
    across_core.wait()
    own_others(2 - 2 * e + 1 - c)

    def meet(met, acc, counts):
        acc[...] = jnp.zeros_like(acc)

        def tile(t, carry):
            member, part = t // 2, pl.multiple_of((t % 2) * TILE, TILE)
            terms = similarity(met[...], own[member, pl.ds(part, TILE), :])
            acc[...] += terms[:, :128] + terms[:, 128:]
            sums = jnp.sum(terms.reshape(ROWS // 8, 8, TILE), axis=0)
            if counts is not None:
                row_acc[member, :, pl.ds(part, TILE)] = jnp.where(counts, sums, 0.0)
            else:
                row_acc[member, :, pl.ds(part, TILE)] += sums
            return carry

        lax.fori_loop(0, 4 * ROWS // TILE, tile, 0)

    drain(stage2.at[pl.ds(0, GROUPS - 1)], recv2)
    pair = at(y, xx + 1 - 2 * (xx % 2), h)
    for i in range(2):
        columns = pl.ds(pl.multiple_of(i * 512 + half, 256), 256)
        remote(met2.at[:, columns], met2.at[:, columns], fwd_send.at[i], fwd_recv.at[i], pair).start()
    for i in range(2):
        columns = pl.ds(pl.multiple_of(i * 512 + half, 256), 256)
        remote(met2.at[:, columns], met2.at[:, columns], fwd_send.at[i], fwd_recv.at[i], pair).wait()
    meet(met2, acc2, receives(blk))

    drain(stage1.at[pl.ds(0, GROUPS - 1)], recv1)
    meet(met1, acc1, None)

    siblings = []
    for i in (1, 2, 3):
        member = (grp + i) % 4
        copy = remote(
            row_acc.at[member], row_in.at[i - 1], row_send.at[i - 1], row_recv.at[i - 1], (blk, member)
        )
        copy.start()
        siblings.append(copy)
    for u, acc in ((0, acc1), (1, acc2)):
        sums = lane_sums(acc[...])
        for s in range(4):
            col_out[s // 2, u * 2 + s % 2, :] = sums[0, s * 128 : (s + 1) * 128]
    line = []
    for i in range(1, 8):
        th, te = (h + i // 2) % 4, (e + i) % 2
        copy = remote(
            col_out.at[te], col_all.at[xx, y, 2 * h + e], col_send.at[0], col_recv.at[0], at(y, xx, th, te)
        )
        copy.start()
    col_all[xx, y, 2 * h + e] = col_out[e]
    own_sums = lane_sums(own_acc[...])[0:1, :]
    drain(col_all.at[0, 0, pl.ds(0, 7)], col_recv.at[0])
    for i in (1, 2, 3):
        remote(
            col_all.at[xx, y], col_all.at[xx, y], col_send.at[1], col_recv.at[1], at(y + i, xx, h)
        ).start()
    for copy in siblings:
        copy.wait()
    total = row_acc[grp] + row_in[0] + row_in[1] + row_in[2]
    density = jnp.sum(total, axis=0, keepdims=True) + own_sums
    drain(col_all.at[0, pl.ds(0, 3)], col_recv.at[1])
    for i in (1, 2, 3):
        remote(col_all.at[xx], col_all.at[xx], col_send.at[2], col_recv.at[2], at(y, xx + i, h)).start()
    drain(col_all.at[pl.ds(0, 3)], col_recv.at[2])

    a1 = jnp.where(first(blk), partners[1, blk], partners[0, blk])
    a2 = partners[2, blk]
    silent = jnp.logical_not(receives(blk))

    def column_sums(a, u, q):
        ay, ax, ah = a // 16, (a // 4) % 4, a % 4
        d = (ah - q + 4) % 4
        j0 = jnp.where(d == 2, 3, jnp.where(d == 3, 2, d))
        j1 = jnp.where(d == 0, 2, jnp.where(d == 3, 3, d - 1))
        j = jnp.where(e == 0, j0, j1)
        return col_all[ax, ay, 2 * ah + j // 2, pl.ds(u * 2 + j % 2, 1), :]

    for q in range(4):
        part = density[:, q * 128 : (q + 1) * 128] + column_sums(a1, 0, q)
        part = part + jnp.where(silent, column_sums(a2, 1, q), 0.0)
        out[pl.ds(q, 1), :] = part

    drain(pieces.at[pl.ds(0, GROUPS - 1)], spread_send)
    drain(stage1.at[pl.ds(0, GROUPS - 1)], send1)
    drain(stage2.at[pl.ds(0, GROUPS - 1)], send2)
    drain(col_all.at[0, 0, pl.ds(0, 7)], col_send.at[0])
    drain(col_all.at[0, pl.ds(0, 3)], col_send.at[1])
    drain(col_all.at[pl.ds(0, 3)], col_send.at[2])


def body(embeddings, partners):
    f32, bf16, dma = jnp.float32, jnp.bfloat16, pltpu.SemaphoreType.DMA
    regular = pltpu.SemaphoreType.REGULAR
    density = pl.pallas_call(
        kernel,
        out_shape=jax.ShapeDtypeStruct((4, 128), f32),
        in_specs=[
            pl.BlockSpec(memory_space=pltpu.SMEM),
            pl.BlockSpec(memory_space=pltpu.VMEM),
        ],
        out_specs=pl.BlockSpec(memory_space=pltpu.VMEM),
        scratch_shapes=[
            pltpu.VMEM((4, ROWS, WIDTH), bf16),
            pltpu.VMEM((GROUPS, 16, 512), bf16),
            pltpu.VMEM((GROUPS, 16, 512), bf16),
            pltpu.VMEM((GROUPS, 16, 256), bf16),
            pltpu.VMEM((ROWS, WIDTH), bf16),
            pltpu.VMEM((ROWS, WIDTH), bf16),
            pltpu.VMEM((ROWS, 128), f32),
            pltpu.VMEM((ROWS, 128), f32),
            pltpu.VMEM((ROWS, 128), f32),
            pltpu.VMEM((4, 8, ROWS), f32),
            pltpu.VMEM((3, 8, ROWS), f32),
            pltpu.VMEM((2, 4, 128), f32),
            pltpu.VMEM((4, 4, 8, 4, 128), f32),
            pltpu.SMEM((2, GROUPS), jnp.int32),
            pltpu.SMEM((GROUPS,), jnp.int32),
            pltpu.SMEM((2, GROUPS), jnp.int32),
            pltpu.SMEM((GROUPS,), jnp.int32),
            pltpu.SMEM((GROUPS,), jnp.int32),
            pltpu.SMEM((GROUPS,), jnp.int32),
            regular, regular, regular,
            dma, dma, dma, dma, dma, dma,
            dma((3,)), dma((3,)), dma((2,)), dma((2,)), dma((3,)), dma((3,)), dma((3,)), dma((3,)),
        ],
        compiler_params=pltpu.CompilerParams(
            collective_id=0, has_side_effects=True, vmem_limit_bytes=40 * 2**20
        ),
        cost_estimate=pl.CostEstimate(
            flops=2 * 4 * ROWS * 3 * ROWS * WIDTH, bytes_accessed=2**20, transcendentals=12 * ROWS * ROWS
        ),
    )(partners, embeddings)
    return density.reshape(ROWS)


def solution(mesh):
    return jax.shard_map(
        body,
        mesh=mesh,
        in_specs=(P(("blk", "grp"), None), P()),
        out_specs=P(("blk", "grp")),
        check_vma=False,
    )
```

time: 310 us -> 116 us (0.37)
  blocking collectives: 135 us -> 0 us
  waiting for transfers between devices: 120 us -> 0 us
  Pallas kernels: 0 us -> 114 us
  matrix products: 19.9 us -> 0 us
  starting transfers between devices: 14.7 us -> 0 us
  between operations: 13.3 us -> 0.01 us
    all_to_all x3 -> x0, blocking collectives: 135 us -> none  [body(): lax.all_to_all(outgoing, 'blk', split_axis=0, concat_axis=0, tiled=True)]
    pallas_call x0 -> x1, Pallas kernels: none -> 114 us  [body(): pl.pallas_call(kernel, out_shape=jax.ShapeDtypeStruct((4, 128), f32), in_...]
    all_gather x4 -> x0, waiting for transfers between devices: 81 us -> none  [the longest x3 81 us: body(): lax.all_gather(routed[turn_index], 'grp', axis=0, tiled=True)]
    all_to_all x1 -> x0, waiting for transfers between devices: 38.7 us -> none  [body(): lax.all_to_all(embeddings.reshape(block_list, row_count // block_list, fe...]
    dot_general x4 -> x0, matrix products: 19.9 us -> none  [scorer(): lax.dot_general(members, columns, (((1,), (1,)), ((), ())), preferred_ele...]
    all_to_all x1 -> x0, starting transfers between devices: 14.6 us -> none  [body(): lax.all_to_all(embeddings.reshape(block_list, row_count // block_list, fe...]
  transfers between devices with their start and end apart: 5 -> 0, of which waited for: 3 -> 0; matrix products, arithmetic and copies ran while one was open for 6% -> 0% of each run, Pallas kernels for 0% -> 0%
where the time goes in v1:
time: 116 us
  Pallas kernels  114 us (98%)
  local copies, waits for them, and re-layouts  2.49 us (2%)
    pallas_call x1, Pallas kernels, body(): pl.pallas_call(kernel, out_shape=jax.ShapeDtypeStruct((4, 128), f32), in_...  114 us
    unnamed x5, local copies, waits for them, and re-layouts  2.49 us

profile of v1, /device:TPU:8, one launch (start us, length us, event | category | flops | bytes accessed | tf_op | source)
XLA Modules:
  0.0 116.3 jit_solution(13615909210795720440)
XLA Ops:
  0.0 0.0 copy-start
  0.0 1.2 %copy-done = bf16[512,1024]{1,0:T(8,128)(2,1)S(1)} copy-done((bf16[512,1024]{1,0:T(8,128)(2,1)S(1)}, bf16[512,1024]{1,0:T(8,128)(2,1)}, u32[]{:S(2)}) %copy-start) | copy-done | bytes 1048600
  1.2 0.0 copy-start.1
  1.2 0.7 copy-done.1
  1.9 113.8 %shard_map.28 = f32[4,128]{1,0:T(4,128)S(1)} custom-call(s32[3,64]{1,0:T(4,128)S(1)} %copy-done.1, bf16[512,1024]{1,0:T(8,128)(2,1)S(1)} %copy-done), custom_call_target="tpu_custom_call" | custom-call | flops 6442450944 | bytes 1048576 | tf_op jit(solution)/shard_map/pallas_call | solution.py:297
  115.7 0.6 copy.4
Async XLA Ops:
  0.0 1.2 %copy-start = (bf16[512,1024]{1,0:T(8,128)(2,1)S(1)}, bf16[512,1024]{1,0:T(8,128)(2,1)}, u32[]{:S(2)}) copy-start(bf16[512,1024]{1,0:T(8,128)(2,1)} %x.1) | copy-start | bytes 3145732
  1.2 0.7 copy-start.1

commit v2 on v1

--- a/solution.py
+++ b/solution.py
@@ -30,11 +30,11 @@
 
 
 def kernel(
-    partners, x, out,
+    rounds, rows, out,
     own, pieces, stage1, stage2, met1, met2, own_acc, acc1, acc2, row_acc, row_in, col_out, col_all,
-    hop_a, low_a, hop_b, low_b, pick1, pick2,
+    partners, hop_a, low_a, hop_b, low_b, pick1, pick2,
     line_y, line_z, other, spread_send, spread_recv, send1, recv1, send2, recv2,
-    own_send, own_recv, fwd_send, fwd_recv, row_send, row_recv, col_send, col_recv,
+    load, table, own_send, own_recv, fwd_send, fwd_recv, row_send, row_recv, col_send, col_recv,
 ):
     blk, grp = lax.axis_index("blk"), lax.axis_index("grp")
     y, xx, h = blk // 16, (blk // 4) % 4, blk % 4
@@ -55,6 +55,28 @@
 
     def drain(ref, sem):
         pltpu.make_async_copy(ref, ref, sem).wait()
+
+    x = own.at[grp]
+    fetch = pltpu.make_async_copy(rows, x, load)
+    fetch.start()
+    fetch_table = pltpu.make_async_copy(rounds, partners, table)
+    fetch_table.start()
+
+    def spread(dy, dx, dh):
+        ty, tx, th = (y + dy) % 4, (xx + dx) % 4, (h + dh) % 4
+        row = pl.multiple_of((th * 8 + ty * 2 + tx // 2) * 16, 16)
+        col = pl.multiple_of((tx % 2) * 512, 512)
+        remote(
+            x.at[pl.ds(row, 16), pl.ds(col, 512)], pieces.at[blk], spread_send, spread_recv, at(ty, tx, th)
+        ).start()
+
+    def spread_plane(j, carry):
+        spread(1 + j // 3, 1 + j % 3, 0)
+        return carry
+
+    def spread_rest(j, carry):
+        spread((1 + j // 3) // 4, (1 + j // 3) % 4, 1 + j % 3)
+        return carry
 
     barrier = pltpu.get_barrier_semaphore()
     for i in (1, 2, 3):
@@ -64,26 +86,29 @@
     signal(barrier, at(y, xx, h, 1 - e))
     signal(barrier, at(y, xx, h, e, 1 - c))
     signal(barrier, at(y, xx, h, 1 - e, 1 - c))
+    fetch.wait()
     pl.semaphore_wait(barrier, 12)
-    own_core = remote(x, own.at[grp], own_send.at[0], own_recv.at[0], at(y, xx, h, e, 1 - c))
+    for i in (1, 2, 3):
+        signal(line_y, at(y + i, xx, h))
+
+    def own_chip(i):
+        part = own.at[grp, pl.ds(i * TILE, TILE)]
+        return remote(part, part, own_send.at[1 + i], own_recv.at[1 + i], at(y, xx, h, 1 - e))
+
+    own_chip(0).start()
+    for i in (1, 2, 3):
+        spread(0, 0, i)
+        spread(i, 0, 0)
+        spread(0, i, 0)
+    pl.semaphore_wait(line_y, 3)
+    for i in (1, 2, 3):
+        signal(line_z, at(y, xx, h + i))
+    lax.fori_loop(0, 9, spread_plane, 0)
+    pl.semaphore_wait(line_z, 3)
+    signal(other, at(y, xx, h, 1 - e))
+    lax.fori_loop(0, 45, spread_rest, 0)
+    own_core = remote(x, x, own_send.at[0], own_recv.at[0], at(y, xx, h, e, 1 - c))
     own_core.start()
-    for i in (1, 2, 3):
-        signal(line_y, at(y + i, xx, h))
-    pl.semaphore_wait(line_y, 3)
-    for i in (1, 2, 3):
-        signal(line_z, at(y, xx, h + i))
-    pl.semaphore_wait(line_z, 3)
-
-    def spread(k, carry):
-        ty, tx, th = (y + k // 16) % 4, (xx + (k // 4) % 4) % 4, (h + k) % 4
-        row = pl.multiple_of((th * 8 + ty * 2 + tx // 2) * 16, 16)
-        col = pl.multiple_of((tx % 2) * 512, 512)
-        remote(
-            x.at[pl.ds(row, 16), pl.ds(col, 512)], pieces.at[blk], spread_send, spread_recv, at(ty, tx, th)
-        ).start()
-        return carry
-
-    lax.fori_loop(1, GROUPS, spread, 0)
     my_row = pl.multiple_of((h * 8 + y * 2 + xx // 2) * 16, 16)
     my_col = pl.multiple_of((xx % 2) * 512, 512)
     pieces[blk] = x[pl.ds(my_row, 16), pl.ds(my_col, 512)]
@@ -98,6 +123,7 @@
         low_b[g] = g
         return carry
 
+    fetch_table.wait()
     lax.fori_loop(0, GROUPS, begin, 0)
     for step in range(5):
         now, later = step % 2, (step + 1) % 2
@@ -129,32 +155,22 @@
     diagonal = lax.broadcasted_iota(jnp.int32, (ROWS, TILE), 0)
     across = lax.broadcasted_iota(jnp.int32, (ROWS, TILE), 1)
 
-    def own_tile(t, carry):
-        start = pl.multiple_of(t * TILE, TILE)
-        block = x[pl.ds(start, TILE), :]
-        own[grp, pl.ds(start, TILE), :] = block
-        terms = jnp.where(diagonal == across + t * TILE, 0.0, similarity(x[...], block))
+    for t in range(ROWS // TILE):
+        terms = similarity(x[...], x[t * TILE : (t + 1) * TILE, :])
+        terms = jnp.where(diagonal == across + t * TILE, 0.0, terms)
         own_acc[...] += terms[:, :128] + terms[:, 128:]
-        return carry
-
-    lax.fori_loop(0, ROWS // TILE, own_tile, 0)
 
     def own_others(member):
-        def tile(t, carry):
-            terms = similarity(x[...], own[member, pl.ds(pl.multiple_of(t * TILE, TILE), TILE), :])
+        for t in range(ROWS // TILE):
+            terms = similarity(x[...], own[member, t * TILE : (t + 1) * TILE, :])
             own_acc[...] += terms[:, :128] + terms[:, 128:]
-            return carry
-
-        lax.fori_loop(0, ROWS // TILE, tile, 0)
 
     own_core.wait()
     own_others(e * 2 + 1 - c)
 
     drain(pieces.at[pl.ds(0, GROUPS - 1)], spread_recv)
-    signal(other, at(y, xx, h, 1 - e))
     pl.semaphore_wait(other, 1)
-    own_chip = remote(x, own.at[grp], own_send.at[1], own_recv.at[1], at(y, xx, h, 1 - e))
-    own_chip.start()
+    own_chip(1).start()
 
     def place(k):
         d = k % 4
@@ -193,36 +209,33 @@
         pick2[blk], :, pl.ds(half, 256)
     ]
 
-    own_chip.wait()
+    def meet(met, acc, counts):
+        acc[...] = jnp.zeros_like(acc)
+
+        for t in range(4 * ROWS // TILE):
+            member, part = t // 2, slice((t % 2) * TILE, (t % 2 + 1) * TILE)
+            terms = similarity(met[...], own[member, part, :])
+            acc[...] += terms[:, :128] + terms[:, 128:]
+            sums = jnp.sum(terms.reshape(ROWS // 8, 8, TILE), axis=0)
+            if counts is not None:
+                row_acc[member, :, part] = jnp.where(counts, sums, 0.0)
+            else:
+                row_acc[member, :, part] += sums
+
+    drain(stage2.at[pl.ds(0, GROUPS - 1)], recv2)
+    pair = at(y, xx + 1 - 2 * (xx % 2), h)
+    for i in range(2):
+        columns = pl.ds(pl.multiple_of(i * 512 + half, 256), 256)
+        remote(met2.at[:, columns], met2.at[:, columns], fwd_send.at[i], fwd_recv.at[i], pair).start()
+    own_chip(0).wait()
+    own_chip(1).wait()
     across_core = remote(
-        own.at[2 - 2 * e + c], own.at[2 - 2 * e + c], own_send.at[2], own_recv.at[2], at(y, xx, h, e, 1 - c)
+        own.at[2 - 2 * e + c], own.at[2 - 2 * e + c], own_send.at[3], own_recv.at[3], at(y, xx, h, e, 1 - c)
     )
     across_core.start()
     own_others(2 - 2 * e + c)
     across_core.wait()
     own_others(2 - 2 * e + 1 - c)
-
-    def meet(met, acc, counts):
-        acc[...] = jnp.zeros_like(acc)
-
-        def tile(t, carry):
-            member, part = t // 2, pl.multiple_of((t % 2) * TILE, TILE)
-            terms = similarity(met[...], own[member, pl.ds(part, TILE), :])
-            acc[...] += terms[:, :128] + terms[:, 128:]
-            sums = jnp.sum(terms.reshape(ROWS // 8, 8, TILE), axis=0)
-            if counts is not None:
-                row_acc[member, :, pl.ds(part, TILE)] = jnp.where(counts, sums, 0.0)
-            else:
-                row_acc[member, :, pl.ds(part, TILE)] += sums
-            return carry
-
-        lax.fori_loop(0, 4 * ROWS // TILE, tile, 0)
-
-    drain(stage2.at[pl.ds(0, GROUPS - 1)], recv2)
-    pair = at(y, xx + 1 - 2 * (xx % 2), h)
-    for i in range(2):
-        columns = pl.ds(pl.multiple_of(i * 512 + half, 256), 256)
-        remote(met2.at[:, columns], met2.at[:, columns], fwd_send.at[i], fwd_recv.at[i], pair).start()
     for i in range(2):
         columns = pl.ds(pl.multiple_of(i * 512 + half, 256), 256)
         remote(met2.at[:, columns], met2.at[:, columns], fwd_send.at[i], fwd_recv.at[i], pair).wait()
@@ -298,8 +311,8 @@
         kernel,
         out_shape=jax.ShapeDtypeStruct((4, 128), f32),
         in_specs=[
-            pl.BlockSpec(memory_space=pltpu.SMEM),
-            pl.BlockSpec(memory_space=pltpu.VMEM),
+            pl.BlockSpec(memory_space=pl.ANY),
+            pl.BlockSpec(memory_space=pl.ANY),
         ],
         out_specs=pl.BlockSpec(memory_space=pltpu.VMEM),
         scratch_shapes=[
@@ -316,6 +329,7 @@
             pltpu.VMEM((3, 8, ROWS), f32),
             pltpu.VMEM((2, 4, 128), f32),
             pltpu.VMEM((4, 4, 8, 4, 128), f32),
+            pltpu.SMEM((3, GROUPS), jnp.int32),
             pltpu.SMEM((2, GROUPS), jnp.int32),
             pltpu.SMEM((GROUPS,), jnp.int32),
             pltpu.SMEM((2, GROUPS), jnp.int32),
@@ -324,10 +338,10 @@
             pltpu.SMEM((GROUPS,), jnp.int32),
             regular, regular, regular,
             dma, dma, dma, dma, dma, dma,
-            dma((3,)), dma((3,)), dma((2,)), dma((2,)), dma((3,)), dma((3,)), dma((3,)), dma((3,)),
+            dma, dma, dma((4,)), dma((4,)), dma((2,)), dma((2,)), dma((3,)), dma((3,)), dma((3,)), dma((3,)),
         ],
         compiler_params=pltpu.CompilerParams(
-            collective_id=0, has_side_effects=True, vmem_limit_bytes=40 * 2**20
+            collective_id=0, has_side_effects=True, vmem_limit_bytes=60 * 2**20
         ),
         cost_estimate=pl.CostEstimate(
             flops=2 * 4 * ROWS * 3 * ROWS * WIDTH, bytes_accessed=2**20, transcendentals=12 * ROWS * ROWS

time: 116 us -> 106 us (0.914)
  Pallas kernels: 114 us -> 105 us
  local copies, waits for them, and re-layouts: 2.49 us -> 1.26 us
    pallas_call x1, Pallas kernels: 114 us -> 105 us  [body(): pl.pallas_call(kernel, out_shape=jax.ShapeDtypeStruct((4, 128), f32), in_...]
    unnamed x5 -> x1, local copies, waits for them, and re-layouts: 2.49 us -> 1.26 us
where the time goes in v2:
time: 106 us
  Pallas kernels  105 us (99%)
  local copies, waits for them, and re-layouts  1.26 us (1%)
    pallas_call x1, Pallas kernels, body(): pl.pallas_call(kernel, out_shape=jax.ShapeDtypeStruct((4, 128), f32), in_...  105 us

profile of v2, /device:TPU:8, one launch (start us, length us, event | category | flops | bytes accessed | tf_op | source)
XLA Modules:
  0.0 105.9 jit_solution(1233356512550073119)
XLA Ops:
  0.0 104.7 %shard_map.28 = f32[4,128]{1,0:T(4,128)} custom-call(s32[3,64]{1,0:T(4,128)} %rounds.1, bf16[512,1024]{1,0:T(8,128)(2,1)} %rows.1), custom_call_target="tpu_custom_call" | custom-call | flops 6442450944 | bytes 1048576 | tf_op jit(solution)/shard_map/pallas_call | solution.py:310
  104.7 1.3 %copy.4 = f32[512]{0:T(512)} copy(f32[512]{0:T(512)} %bitcast.1) | data formatting | bytes 4096

commit v3 on v2

--- a/solution.py
+++ b/solution.py
@@ -14,6 +14,9 @@
 ROWS = 512
 WIDTH = 1024
 TILE = 256
+CHUNK = 16
+FEW, MANY = 7, 21
+EARLY = ROWS - CHUNK * (FEW + MANY)
 
 
 def similarity(columns, members):
@@ -31,8 +34,8 @@
 
 def kernel(
     rounds, rows, out,
-    own, pieces, stage1, stage2, met1, met2, own_acc, acc1, acc2, row_acc, row_in, col_out, col_all,
-    partners, hop_a, low_a, hop_b, low_b, pick1, pick2,
+    own, pieces, stage1, stage2, met1, met2, own_acc, acc1, acc2, row_acc, row_in, col_out, col_line, col_stage, col_plane,
+    partners, hop_a, low_a, hop_b, low_b, pick1, pick2, back,
     line_y, line_z, other, spread_send, spread_recv, send1, recv1, send2, recv2,
     load, table, own_send, own_recv, fwd_send, fwd_recv, row_send, row_recv, col_send, col_recv,
 ):
@@ -91,11 +94,11 @@
     for i in (1, 2, 3):
         signal(line_y, at(y + i, xx, h))
 
-    def own_chip(i):
-        part = own.at[grp, pl.ds(i * TILE, TILE)]
+    def own_chip(i, start, size):
+        part = own.at[grp, pl.ds(start, size)]
         return remote(part, part, own_send.at[1 + i], own_recv.at[1 + i], at(y, xx, h, 1 - e))
 
-    own_chip(0).start()
+    own_chip(0, 0, EARLY).start()
     for i in (1, 2, 3):
         spread(0, 0, i)
         spread(i, 0, 0)
@@ -146,6 +149,7 @@
 
     def choose(g, carry):
         pick1[g] = jnp.where(first(g), partners[0, g], partners[1, g])
+        back[g] = jnp.where(first(g), partners[1, g], partners[0, g])
         pick2[g] = partners[2, jnp.where(receives(g), g, mate(g))]
         return carry
 
@@ -170,7 +174,6 @@
 
     drain(pieces.at[pl.ds(0, GROUPS - 1)], spread_recv)
     pl.semaphore_wait(other, 1)
-    own_chip(1).start()
 
     def place(k):
         d = k % 4
@@ -200,8 +203,16 @@
         ).start()
         return carry
 
-    lax.fori_loop(1, GROUPS, half_units, 0)
-    lax.fori_loop(1, GROUPS, units, 0)
+    def paced(send, count, first_row):
+        def group(i, carry):
+            own_chip(1, pl.multiple_of(first_row + i * CHUNK, CHUNK), CHUNK).start()
+            per = (GROUPS - 1) // count
+            return lax.fori_loop(1 + i * per, 1 + (i + 1) * per, send, carry)
+
+        lax.fori_loop(0, count, group, 0)
+
+    paced(half_units, FEW, EARLY)
+    paced(units, MANY, EARLY + FEW * CHUNK)
     home = pl.multiple_of((2 * e + 0) * 128 + (y * 2 + xx // 2) * 16, 16)
     half = pl.multiple_of((xx % 2) * 256, 256)
     met1[pl.ds(home, 16), pl.ds(my_col, 512)] = pieces[pick1[blk]]
@@ -227,8 +238,8 @@
     for i in range(2):
         columns = pl.ds(pl.multiple_of(i * 512 + half, 256), 256)
         remote(met2.at[:, columns], met2.at[:, columns], fwd_send.at[i], fwd_recv.at[i], pair).start()
-    own_chip(0).wait()
-    own_chip(1).wait()
+    own_chip(0, 0, EARLY).wait()
+    own_chip(1, EARLY, ROWS - EARLY).wait()
     across_core = remote(
         own.at[2 - 2 * e + c], own.at[2 - 2 * e + c], own_send.at[3], own_recv.at[3], at(y, xx, h, e, 1 - c)
     )
@@ -241,9 +252,24 @@
         remote(met2.at[:, columns], met2.at[:, columns], fwd_send.at[i], fwd_recv.at[i], pair).wait()
     meet(met2, acc2, receives(blk))
 
+    def publish(u, acc):
+        sums = lane_sums(acc[...])
+        for s in range(4):
+            col_out[s // 2, u, pl.ds(s % 2, 1), :] = sums[0:1, s * 128 : (s + 1) * 128]
+
+    publish(1, acc2)
+    own_sums = lane_sums(own_acc[...])[0:1, :]
+
     drain(stage1.at[pl.ds(0, GROUPS - 1)], recv1)
     meet(met1, acc1, None)
 
+    publish(0, acc1)
+    for i in range(1, 8):
+        th, te = (h + i // 2) % 4, (e + i) % 2
+        remote(
+            col_out.at[te], col_line.at[2 * h + e], col_send.at[0], col_recv.at[0], at(y, xx, th, te)
+        ).start()
+    col_line[2 * h + e] = col_out[e]
     siblings = []
     for i in (1, 2, 3):
         member = (grp + i) % 4
@@ -252,56 +278,50 @@
         )
         copy.start()
         siblings.append(copy)
-    for u, acc in ((0, acc1), (1, acc2)):
-        sums = lane_sums(acc[...])
-        for s in range(4):
-            col_out[s // 2, u * 2 + s % 2, :] = sums[0, s * 128 : (s + 1) * 128]
-    line = []
-    for i in range(1, 8):
-        th, te = (h + i // 2) % 4, (e + i) % 2
-        copy = remote(
-            col_out.at[te], col_all.at[xx, y, 2 * h + e], col_send.at[0], col_recv.at[0], at(y, xx, th, te)
-        )
-        copy.start()
-    col_all[xx, y, 2 * h + e] = col_out[e]
-    own_sums = lane_sums(own_acc[...])[0:1, :]
-    drain(col_all.at[0, 0, pl.ds(0, 7)], col_recv.at[0])
-    for i in (1, 2, 3):
-        remote(
-            col_all.at[xx, y], col_all.at[xx, y], col_send.at[1], col_recv.at[1], at(y + i, xx, h)
-        ).start()
+    drain(col_line.at[pl.ds(0, 7)], col_recv.at[0])
+
+    def give(k):
+        ty, tx = (y + k // 4) % 4, (xx + k % 4) % 4
+        other_blk = ty * 16 + tx * 4 + h
+        for u, a in ((0, back[other_blk]), (1, partners[2, other_blk])):
+            for i in range(2):
+                col_stage[k, u, i] = col_line[2 * (a % 4) + i, u]
+        return ty, tx
+
+    def give_peer(k, carry):
+        ty, tx = give(k)
+        remote(
+            col_stage.at[k], col_plane.at[y * 4 + xx], col_send.at[1], col_recv.at[1], at(ty, tx, h)
+        ).start()
+        return carry
+
+    lax.fori_loop(1, 16, give_peer, 0)
+    give(0)
+    col_plane[y * 4 + xx] = col_stage[0]
     for copy in siblings:
         copy.wait()
     total = row_acc[grp] + row_in[0] + row_in[1] + row_in[2]
     density = jnp.sum(total, axis=0, keepdims=True) + own_sums
-    drain(col_all.at[0, pl.ds(0, 3)], col_recv.at[1])
-    for i in (1, 2, 3):
-        remote(col_all.at[xx], col_all.at[xx], col_send.at[2], col_recv.at[2], at(y, xx + i, h)).start()
-    drain(col_all.at[pl.ds(0, 3)], col_recv.at[2])
-
-    a1 = jnp.where(first(blk), partners[1, blk], partners[0, blk])
-    a2 = partners[2, blk]
+    drain(col_plane.at[pl.ds(0, 15)], col_recv.at[1])
     silent = jnp.logical_not(receives(blk))
 
     def column_sums(a, u, q):
-        ay, ax, ah = a // 16, (a // 4) % 4, a % 4
-        d = (ah - q + 4) % 4
+        d = (a % 4 - q + 4) % 4
         j0 = jnp.where(d == 2, 3, jnp.where(d == 3, 2, d))
         j1 = jnp.where(d == 0, 2, jnp.where(d == 3, 3, d - 1))
         j = jnp.where(e == 0, j0, j1)
-        return col_all[ax, ay, 2 * ah + j // 2, pl.ds(u * 2 + j % 2, 1), :]
+        return col_plane[a // 4, u, j // 2, pl.ds(j % 2, 1), :]
 
     for q in range(4):
-        part = density[:, q * 128 : (q + 1) * 128] + column_sums(a1, 0, q)
-        part = part + jnp.where(silent, column_sums(a2, 1, q), 0.0)
+        part = density[:, q * 128 : (q + 1) * 128] + column_sums(back[blk], 0, q)
+        part = part + jnp.where(silent, column_sums(partners[2, blk], 1, q), 0.0)
         out[pl.ds(q, 1), :] = part
 
     drain(pieces.at[pl.ds(0, GROUPS - 1)], spread_send)
     drain(stage1.at[pl.ds(0, GROUPS - 1)], send1)
     drain(stage2.at[pl.ds(0, GROUPS - 1)], send2)
-    drain(col_all.at[0, 0, pl.ds(0, 7)], col_send.at[0])
-    drain(col_all.at[0, pl.ds(0, 3)], col_send.at[1])
-    drain(col_all.at[pl.ds(0, 3)], col_send.at[2])
+    drain(col_line.at[pl.ds(0, 7)], col_send.at[0])
+    drain(col_plane.at[pl.ds(0, 15)], col_send.at[1])
 
 
 def body(embeddings, partners):
@@ -327,8 +347,10 @@
             pltpu.VMEM((ROWS, 128), f32),
             pltpu.VMEM((4, 8, ROWS), f32),
             pltpu.VMEM((3, 8, ROWS), f32),
-            pltpu.VMEM((2, 4, 128), f32),
-            pltpu.VMEM((4, 4, 8, 4, 128), f32),
+            pltpu.VMEM((2, 2, 2, 128), f32),
+            pltpu.VMEM((8, 2, 2, 128), f32),
+            pltpu.VMEM((16, 2, 2, 2, 128), f32),
+            pltpu.VMEM((16, 2, 2, 2, 128), f32),
             pltpu.SMEM((3, GROUPS), jnp.int32),
             pltpu.SMEM((2, GROUPS), jnp.int32),
             pltpu.SMEM((GROUPS,), jnp.int32),
@@ -336,9 +358,10 @@
             pltpu.SMEM((GROUPS,), jnp.int32),
             pltpu.SMEM((GROUPS,), jnp.int32),
             pltpu.SMEM((GROUPS,), jnp.int32),
+            pltpu.SMEM((GROUPS,), jnp.int32),
             regular, regular, regular,
             dma, dma, dma, dma, dma, dma,
-            dma, dma, dma((4,)), dma((4,)), dma((2,)), dma((2,)), dma((3,)), dma((3,)), dma((3,)), dma((3,)),
+            dma, dma, dma((4,)), dma((4,)), dma((2,)), dma((2,)), dma((3,)), dma((3,)), dma((2,)), dma((2,)),
         ],
         compiler_params=pltpu.CompilerParams(
             collective_id=0, has_side_effects=True, vmem_limit_bytes=60 * 2**20

time: 106 us -> 96.6 us (0.911); the launches traced: 106 us -> 95.4 us
  Pallas kernels: 105 us -> 94.2 us
    pallas_call x1, Pallas kernels: 105 us -> 94.2 us  [body(): pl.pallas_call(kernel, out_shape=jax.ShapeDtypeStruct((4, 128), f32), in_...]
where the time goes in v3:
time: 96.6 us; the launch traced here: 95.4 us
  Pallas kernels  94.2 us (98%)
  local copies, waits for them, and re-layouts  1.26 us (1%)
    pallas_call x1, Pallas kernels, body(): pl.pallas_call(kernel, out_shape=jax.ShapeDtypeStruct((4, 128), f32), in_...  94.2 us

profile of v3, /device:TPU:8, one launch (start us, length us, event | category | flops | bytes accessed | tf_op | source)
XLA Modules:
  0.0 95.4 jit_solution(17824155871154078045)
XLA Ops:
  0.0 94.2 %shard_map.28 = f32[4,128]{1,0:T(4,128)} custom-call(s32[3,64]{1,0:T(4,128)} %rounds.1, bf16[512,1024]{1,0:T(8,128)(2,1)} %rows.1), custom_call_target="tpu_custom_call" | custom-call | flops 6442450944 | bytes 1048576 | tf_op jit(solution)/shard_map/pallas_call | solution.py:330
  94.2 1.3 %copy.4 = f32[512]{0:T(512)} copy(f32[512]{0:T(512)} %bitcast.1) | data formatting | bytes 4096

commit v4 on v3

--- a/solution.py
+++ b/solution.py
@@ -14,9 +14,9 @@
 ROWS = 512
 WIDTH = 1024
 TILE = 256
-CHUNK = 16
-FEW, MANY = 7, 21
-EARLY = ROWS - CHUNK * (FEW + MANY)
+EARLY = 64
+FEW, FEW_ROWS = 7, 16
+MANY, MANY_ROWS = 21, 16
 
 
 def similarity(columns, members):
@@ -36,7 +36,7 @@
     rounds, rows, out,
     own, pieces, stage1, stage2, met1, met2, own_acc, acc1, acc2, row_acc, row_in, col_out, col_line, col_stage, col_plane,
     partners, hop_a, low_a, hop_b, low_b, pick1, pick2, back,
-    line_y, line_z, other, spread_send, spread_recv, send1, recv1, send2, recv2,
+    line_y, line_h, line_z, other, spread_send, spread_recv, send1, recv1, send2, recv2,
     load, table, own_send, own_recv, fwd_send, fwd_recv, row_send, row_recv, col_send, col_recv,
 ):
     blk, grp = lax.axis_index("blk"), lax.axis_index("grp")
@@ -73,12 +73,17 @@
             x.at[pl.ds(row, 16), pl.ds(col, 512)], pieces.at[blk], spread_send, spread_recv, at(ty, tx, th)
         ).start()
 
+    def spread_lines(j, carry):
+        spread(1 + j // 3, 0, 1 + j % 3)
+        spread(0, 1 + j // 3, 1 + j % 3)
+        return carry
+
     def spread_plane(j, carry):
         spread(1 + j // 3, 1 + j % 3, 0)
         return carry
 
     def spread_rest(j, carry):
-        spread((1 + j // 3) // 4, (1 + j // 3) % 4, 1 + j % 3)
+        spread(1 + j // 9, 1 + (j // 3) % 3, 1 + j % 3)
         return carry
 
     barrier = pltpu.get_barrier_semaphore()
@@ -93,6 +98,7 @@
     pl.semaphore_wait(barrier, 12)
     for i in (1, 2, 3):
         signal(line_y, at(y + i, xx, h))
+        signal(line_h, at(y, xx, h + i))
 
     def own_chip(i, start, size):
         part = own.at[grp, pl.ds(start, size)]
@@ -106,10 +112,12 @@
     pl.semaphore_wait(line_y, 3)
     for i in (1, 2, 3):
         signal(line_z, at(y, xx, h + i))
-    lax.fori_loop(0, 9, spread_plane, 0)
+    pl.semaphore_wait(line_h, 3)
+    lax.fori_loop(0, 9, spread_lines, 0)
     pl.semaphore_wait(line_z, 3)
     signal(other, at(y, xx, h, 1 - e))
-    lax.fori_loop(0, 45, spread_rest, 0)
+    lax.fori_loop(0, 27, spread_rest, 0)
+    lax.fori_loop(0, 9, spread_plane, 0)
     own_core = remote(x, x, own_send.at[0], own_recv.at[0], at(y, xx, h, e, 1 - c))
     own_core.start()
     my_row = pl.multiple_of((h * 8 + y * 2 + xx // 2) * 16, 16)
@@ -203,16 +211,17 @@
         ).start()
         return carry
 
-    def paced(send, count, first_row):
+    def paced(send, count, per, first_row, rows_each):
         def group(i, carry):
-            own_chip(1, pl.multiple_of(first_row + i * CHUNK, CHUNK), CHUNK).start()
-            per = (GROUPS - 1) // count
+            start = pl.multiple_of(first_row + i * rows_each, 16)
+            own_chip(1, start, rows_each).start()
             return lax.fori_loop(1 + i * per, 1 + (i + 1) * per, send, carry)
 
         lax.fori_loop(0, count, group, 0)
 
-    paced(half_units, FEW, EARLY)
-    paced(units, MANY, EARLY + FEW * CHUNK)
+    paced(half_units, FEW, (GROUPS - 1) // FEW, EARLY, FEW_ROWS)
+    paced(units, MANY, 3, EARLY + FEW * FEW_ROWS, MANY_ROWS)
+    lax.fori_loop(1 + 3 * MANY, GROUPS, units, 0)
     home = pl.multiple_of((2 * e + 0) * 128 + (y * 2 + xx // 2) * 16, 16)
     half = pl.multiple_of((xx % 2) * 256, 256)
     met1[pl.ds(home, 16), pl.ds(my_col, 512)] = pieces[pick1[blk]]
@@ -220,11 +229,9 @@
         pick2[blk], :, pl.ds(half, 256)
     ]
 
-    def meet(met, acc, counts):
-        acc[...] = jnp.zeros_like(acc)
-
-        for t in range(4 * ROWS // TILE):
-            member, part = t // 2, slice((t % 2) * TILE, (t % 2 + 1) * TILE)
+    def meet(met, acc, counts, member):
+        for t in range(ROWS // TILE):
+            part = slice(t * TILE, (t + 1) * TILE)
             terms = similarity(met[...], own[member, part, :])
             acc[...] += terms[:, :128] + terms[:, 128:]
             sums = jnp.sum(terms.reshape(ROWS // 8, 8, TILE), axis=0)
@@ -238,6 +245,14 @@
     for i in range(2):
         columns = pl.ds(pl.multiple_of(i * 512 + half, 256), 256)
         remote(met2.at[:, columns], met2.at[:, columns], fwd_send.at[i], fwd_recv.at[i], pair).start()
+    acc1[...] = jnp.zeros_like(acc1)
+    acc2[...] = jnp.zeros_like(acc2)
+    for i in range(2):
+        columns = pl.ds(pl.multiple_of(i * 512 + half, 256), 256)
+        remote(met2.at[:, columns], met2.at[:, columns], fwd_send.at[i], fwd_recv.at[i], pair).wait()
+    counts = receives(blk)
+    meet(met2, acc2, counts, grp)
+    meet(met2, acc2, counts, 2 * e + 1 - c)
     own_chip(0, 0, EARLY).wait()
     own_chip(1, EARLY, ROWS - EARLY).wait()
     across_core = remote(
@@ -245,12 +260,10 @@
     )
     across_core.start()
     own_others(2 - 2 * e + c)
+    meet(met2, acc2, counts, 2 - 2 * e + c)
     across_core.wait()
     own_others(2 - 2 * e + 1 - c)
-    for i in range(2):
-        columns = pl.ds(pl.multiple_of(i * 512 + half, 256), 256)
-        remote(met2.at[:, columns], met2.at[:, columns], fwd_send.at[i], fwd_recv.at[i], pair).wait()
-    meet(met2, acc2, receives(blk))
+    meet(met2, acc2, counts, 2 - 2 * e + 1 - c)
 
     def publish(u, acc):
         sums = lane_sums(acc[...])
@@ -261,7 +274,8 @@
     own_sums = lane_sums(own_acc[...])[0:1, :]
 
     drain(stage1.at[pl.ds(0, GROUPS - 1)], recv1)
-    meet(met1, acc1, None)
+    for member in range(4):
+        meet(met1, acc1, None, member)
 
     publish(0, acc1)
     for i in range(1, 8):
@@ -288,14 +302,14 @@
                 col_stage[k, u, i] = col_line[2 * (a % 4) + i, u]
         return ty, tx
 
-    def give_peer(k, carry):
+    def give_peer(k):
         ty, tx = give(k)
         remote(
             col_stage.at[k], col_plane.at[y * 4 + xx], col_send.at[1], col_recv.at[1], at(ty, tx, h)
         ).start()
-        return carry
-
-    lax.fori_loop(1, 16, give_peer, 0)
+
+    for k in range(1, 16):
+        give_peer(k)
     give(0)
     col_plane[y * 4 + xx] = col_stage[0]
     for copy in siblings:
@@ -359,7 +373,7 @@
             pltpu.SMEM((GROUPS,), jnp.int32),
             pltpu.SMEM((GROUPS,), jnp.int32),
             pltpu.SMEM((GROUPS,), jnp.int32),
-            regular, regular, regular,
+            regular, regular, regular, regular,
             dma, dma, dma, dma, dma, dma,
             dma, dma, dma((4,)), dma((4,)), dma((2,)), dma((2,)), dma((3,)), dma((3,)), dma((2,)), dma((2,)),
         ],

time: 96.6 us -> 94.3 us (0.976)
  Pallas kernels: 94.2 us -> 91.9 us
    pallas_call x1, Pallas kernels: 94.2 us -> 91.9 us  [body(): pl.pallas_call(kernel, out_shape=jax.ShapeDtypeStruct((4, 128), f32), in_...]
where the time goes in v4:
time: 94.3 us; the launch traced here: 93.1 us
  Pallas kernels  91.9 us (97%)
  local copies, waits for them, and re-layouts  1.26 us (1%)
    pallas_call x1, Pallas kernels, body(): pl.pallas_call(kernel, out_shape=jax.ShapeDtypeStruct((4, 128), f32), in_...  91.9 us

profile of v4, /device:TPU:8, one launch (start us, length us, event | category | flops | bytes accessed | tf_op | source)
XLA Modules:
  0.0 93.1 jit_solution(10138542611207404339)
XLA Ops:
  0.0 91.9 %shard_map.28 = f32[4,128]{1,0:T(4,128)} custom-call(s32[3,64]{1,0:T(4,128)} %rounds.1, bf16[512,1024]{1,0:T(8,128)(2,1)} %rows.1), custom_call_target="tpu_custom_call" | custom-call | flops 6442450944 | bytes 1048576 | tf_op jit(solution)/shard_map/pallas_call | solution.py:344
  91.9 1.3 %copy.4 = f32[512]{0:T(512)} copy(f32[512]{0:T(512)} %bitcast.1) | data formatting | bytes 4096

commit v5 on v4

--- a/solution.py
+++ b/solution.py
@@ -15,8 +15,7 @@
 WIDTH = 1024
 TILE = 256
 EARLY = 64
-FEW, FEW_ROWS = 7, 16
-MANY, MANY_ROWS = 21, 16
+PACE = ((7, 16), (21, 16))
 
 
 def similarity(columns, members):
@@ -25,21 +24,19 @@
 
 
 def lane_sums(total):
-    ones = jnp.ones((8, 128), jnp.float32)
-    return lax.dot_general(
-        ones, total, (((1,), (1,)), ((), ())),
-        precision=lax.Precision.HIGHEST, preferred_element_type=jnp.float32,
-    )
+    parts = [jnp.sum(total[s * 128 : (s + 1) * 128].T, axis=0, keepdims=True) for s in range(4)]
+    return jnp.concatenate(parts, axis=1)
 
 
 def kernel(
     rounds, rows, out,
-    own, pieces, stage1, stage2, met1, met2, own_acc, acc1, acc2, row_acc, row_in, col_out, col_line, col_stage, col_plane,
+    own, pieces_a, pieces_b, stage1, stage2, met1, met2, own_acc, acc1, acc2, row_acc, row_in, col_out, col_line, col_stage, col_plane,
     partners, hop_a, low_a, hop_b, low_b, pick1, pick2, back,
     line_y, line_h, line_z, other, spread_send, spread_recv, send1, recv1, send2, recv2,
     load, table, own_send, own_recv, fwd_send, fwd_recv, row_send, row_recv, col_send, col_recv,
 ):
     blk, grp = lax.axis_index("blk"), lax.axis_index("grp")
+    pieces = (pieces_a, pieces_b)
     y, xx, h = blk // 16, (blk // 4) % 4, blk % 4
     e, c = grp // 2, grp % 2
 
@@ -65,12 +62,16 @@
     fetch_table = pltpu.make_async_copy(rounds, partners, table)
     fetch_table.start()
 
-    def spread(dy, dx, dh):
+    def spread(dy, dx, dh, part=0):
         ty, tx, th = (y + dy) % 4, (xx + dx) % 4, (h + dh) % 4
         row = pl.multiple_of((th * 8 + ty * 2 + tx // 2) * 16, 16)
-        col = pl.multiple_of((tx % 2) * 512, 512)
+        col = pl.multiple_of((tx % 2) * 512 + part * 256, 256)
         remote(
-            x.at[pl.ds(row, 16), pl.ds(col, 512)], pieces.at[blk], spread_send, spread_recv, at(ty, tx, th)
+            x.at[pl.ds(row, 16), pl.ds(col, 256)],
+            pieces[part].at[blk],
+            spread_send.at[part],
+            spread_recv.at[part],
+            at(ty, tx, th),
         ).start()
 
     def spread_lines(j, carry):
@@ -118,11 +119,19 @@
     signal(other, at(y, xx, h, 1 - e))
     lax.fori_loop(0, 27, spread_rest, 0)
     lax.fori_loop(0, 9, spread_plane, 0)
+
+    def spread_second(k, carry):
+        spread(k // 16, (k // 4) % 4, k % 4, 1)
+        return carry
+
+    lax.fori_loop(1, GROUPS, spread_second, 0)
     own_core = remote(x, x, own_send.at[0], own_recv.at[0], at(y, xx, h, e, 1 - c))
     own_core.start()
     my_row = pl.multiple_of((h * 8 + y * 2 + xx // 2) * 16, 16)
     my_col = pl.multiple_of((xx % 2) * 512, 512)
-    pieces[blk] = x[pl.ds(my_row, 16), pl.ds(my_col, 512)]
+    for part in range(2):
+        lanes = pl.ds(pl.multiple_of(my_col + part * 256, 256), 256)
+        pieces[part][blk] = x[pl.ds(my_row, 16), lanes]
 
     def mate(g):
         return g + 4 - 8 * ((g // 4) % 2)
@@ -179,9 +188,6 @@
 
     own_core.wait()
     own_others(e * 2 + 1 - c)
-
-    drain(pieces.at[pl.ds(0, GROUPS - 1)], spread_recv)
-    pl.semaphore_wait(other, 1)
 
     def place(k):
         d = k % 4
@@ -193,41 +199,57 @@
         row = pl.multiple_of(slot * 128 + (y * 2 + xx // 2) * 16, 16)
         return ty, tx, th, to, row
 
-    def half_units(k, carry):
-        ty, tx, th, to, row = place(k)
-        lane = pl.multiple_of((tx % 2) * 256, 256)
-        stage2[k] = pieces[pick2[ty * 16 + tx * 4 + th], :, pl.ds(lane, 256)]
-        col = pl.multiple_of((xx % 2) * 512 + (tx % 2) * 256, 256)
-        remote(
-            stage2.at[k], met2.at[pl.ds(row, 16), pl.ds(col, 256)], send2, recv2, at(ty, tx, th, to)
-        ).start()
-        return carry
-
-    def units(k, carry):
-        ty, tx, th, to, row = place(k)
-        stage1[k] = pieces[pick1[ty * 16 + tx * 4 + th]]
-        remote(
-            stage1.at[k], met1.at[pl.ds(row, 16), pl.ds(my_col, 512)], send1, recv1, at(ty, tx, th, to)
-        ).start()
-        return carry
-
-    def paced(send, count, per, first_row, rows_each):
+    half = pl.multiple_of((xx % 2) * 256, 256)
+    home = pl.multiple_of((2 * e + 0) * 128 + (y * 2 + xx // 2) * 16, 16)
+
+    def half_units(part):
+        def send(j, carry):
+            k = (j // 8) * 16 + (2 * ((j // 4) % 2) + (part + xx) % 2) * 4 + j % 4
+            ty, tx, th, to, row = place(k)
+            stage2[k] = pieces[part][pick2[ty * 16 + tx * 4 + th]]
+            col = pl.multiple_of((xx % 2) * 512 + part * 256, 256)
+            remote(
+                stage2.at[k], met2.at[pl.ds(row, 16), pl.ds(col, 256)], send2, recv2, at(ty, tx, th, to)
+            ).start()
+            return carry
+
+        lax.fori_loop(1 - (part + xx) % 2, GROUPS // 2, send, 0)
+
+    def units(part, first_row):
+        count, size = PACE[part]
+        per = (GROUPS - 1) // count
+
+        def send(k, carry):
+            ty, tx, th, to, row = place(k)
+            stage1[part, k] = pieces[part][pick1[ty * 16 + tx * 4 + th]]
+            col = pl.multiple_of(my_col + part * 256, 256)
+            remote(
+                stage1.at[part, k],
+                met1.at[pl.ds(row, 16), pl.ds(col, 256)],
+                send1.at[part],
+                recv1.at[part],
+                at(ty, tx, th, to),
+            ).start()
+            return carry
+
         def group(i, carry):
-            start = pl.multiple_of(first_row + i * rows_each, 16)
-            own_chip(1, start, rows_each).start()
+            own_chip(1, pl.multiple_of(first_row + i * size, 16), size).start()
             return lax.fori_loop(1 + i * per, 1 + (i + 1) * per, send, carry)
 
         lax.fori_loop(0, count, group, 0)
-
-    paced(half_units, FEW, (GROUPS - 1) // FEW, EARLY, FEW_ROWS)
-    paced(units, MANY, 3, EARLY + FEW * FEW_ROWS, MANY_ROWS)
-    lax.fori_loop(1 + 3 * MANY, GROUPS, units, 0)
-    home = pl.multiple_of((2 * e + 0) * 128 + (y * 2 + xx // 2) * 16, 16)
-    half = pl.multiple_of((xx % 2) * 256, 256)
-    met1[pl.ds(home, 16), pl.ds(my_col, 512)] = pieces[pick1[blk]]
-    met2[pl.ds(home, 16), pl.ds(pl.multiple_of(my_col + half, 256), 256)] = pieces[
-        pick2[blk], :, pl.ds(half, 256)
-    ]
+        lax.fori_loop(1 + count * per, GROUPS, send, 0)
+        met1[pl.ds(home, 16), pl.ds(pl.multiple_of(my_col + part * 256, 256), 256)] = pieces[part][pick1[blk]]
+
+    drain(pieces_a.at[pl.ds(0, GROUPS - 1)], spread_recv.at[0])
+    pl.semaphore_wait(other, 1)
+    half_units(0)
+    drain(pieces_b.at[pl.ds(0, GROUPS - 1)], spread_recv.at[1])
+    half_units(1)
+    units(0, EARLY)
+    units(1, EARLY + PACE[0][0] * PACE[0][1])
+    met2[pl.ds(home, 16), pl.ds(pl.multiple_of(my_col + half, 256), 256)] = jnp.where(
+        xx % 2 == 0, pieces_a[pick2[blk]], pieces_b[pick2[blk]]
+    )
 
     def meet(met, acc, counts, member):
         for t in range(ROWS // TILE):
@@ -268,12 +290,13 @@
     def publish(u, acc):
         sums = lane_sums(acc[...])
         for s in range(4):
-            col_out[s // 2, u, pl.ds(s % 2, 1), :] = sums[0:1, s * 128 : (s + 1) * 128]
+            col_out[s // 2, u, pl.ds(s % 2, 1), :] = sums[:, s * 128 : (s + 1) * 128]
 
     publish(1, acc2)
-    own_sums = lane_sums(own_acc[...])[0:1, :]
-
-    drain(stage1.at[pl.ds(0, GROUPS - 1)], recv1)
+    own_sums = lane_sums(own_acc[...])
+
+    drain(stage1.at[0, pl.ds(0, GROUPS - 1)], recv1.at[0])
+    drain(stage1.at[1, pl.ds(0, GROUPS - 1)], recv1.at[1])
     for member in range(4):
         meet(met1, acc1, None, member)
 
@@ -331,8 +354,9 @@
         part = part + jnp.where(silent, column_sums(partners[2, blk], 1, q), 0.0)
         out[pl.ds(q, 1), :] = part
 
-    drain(pieces.at[pl.ds(0, GROUPS - 1)], spread_send)
-    drain(stage1.at[pl.ds(0, GROUPS - 1)], send1)
+    for part in range(2):
+        drain(pieces[part].at[pl.ds(0, GROUPS - 1)], spread_send.at[part])
+        drain(stage1.at[part, pl.ds(0, GROUPS - 1)], send1.at[part])
     drain(stage2.at[pl.ds(0, GROUPS - 1)], send2)
     drain(col_line.at[pl.ds(0, 7)], col_send.at[0])
     drain(col_plane.at[pl.ds(0, 15)], col_send.at[1])
@@ -351,8 +375,9 @@
         out_specs=pl.BlockSpec(memory_space=pltpu.VMEM),
         scratch_shapes=[
             pltpu.VMEM((4, ROWS, WIDTH), bf16),
-            pltpu.VMEM((GROUPS, 16, 512), bf16),
-            pltpu.VMEM((GROUPS, 16, 512), bf16),
+            pltpu.VMEM((GROUPS, 16, 256), bf16),
+            pltpu.VMEM((GROUPS, 16, 256), bf16),
+            pltpu.VMEM((2, GROUPS, 16, 256), bf16),
             pltpu.VMEM((GROUPS, 16, 256), bf16),
             pltpu.VMEM((ROWS, WIDTH), bf16),
             pltpu.VMEM((ROWS, WIDTH), bf16),
@@ -374,7 +399,7 @@
             pltpu.SMEM((GROUPS,), jnp.int32),
             pltpu.SMEM((GROUPS,), jnp.int32),
             regular, regular, regular, regular,
-            dma, dma, dma, dma, dma, dma,
+            dma((2,)), dma((2,)), dma((2,)), dma((2,)), dma, dma,
             dma, dma, dma((4,)), dma((4,)), dma((2,)), dma((2,)), dma((3,)), dma((3,)), dma((2,)), dma((2,)),
         ],
         compiler_params=pltpu.CompilerParams(

time: 94.3 us -> 92.3 us (0.979)
  Pallas kernels: 91.9 us -> 90.7 us
    pallas_call x1, Pallas kernels: 91.9 us -> 90.7 us  [body(): pl.pallas_call(kernel, out_shape=jax.ShapeDtypeStruct((4, 128), f32), in_...]
where the time goes in v5:
time: 92.3 us; the launch traced here: 92 us
  Pallas kernels  90.7 us (98%)
  local copies, waits for them, and re-layouts  1.26 us (1%)
    pallas_call x1, Pallas kernels, body(): pl.pallas_call(kernel, out_shape=jax.ShapeDtypeStruct((4, 128), f32), in_...  90.7 us

profile of v5, /device:TPU:8, one launch (start us, length us, event | category | flops | bytes accessed | tf_op | source)
XLA Modules:
  0.0 92.0 jit_solution(11013468269310684215)
XLA Ops:
  0.0 90.7 %shard_map.28 = f32[4,128]{1,0:T(4,128)} custom-call(s32[3,64]{1,0:T(4,128)} %rounds.1, bf16[512,1024]{1,0:T(8,128)(2,1)} %rows.1), custom_call_target="tpu_custom_call" | custom-call | flops 6442450944 | bytes 1048576 | tf_op jit(solution)/shard_map/pallas_call | solution.py:368
  90.7 1.3 %copy.4 = f32[512]{0:T(512)} copy(f32[512]{0:T(512)} %bitcast.1) | data formatting | bytes 4096

commit v6 on v5

--- a/solution.py
+++ b/solution.py
@@ -23,6 +23,16 @@
     return jnp.exp2(c * RATE - RATE)
 
 
+def half_scores(columns, members, part):
+    c = jnp.zeros((), jnp.float32)
+    for i in range(2):
+        k = slice(i * 512 + part * 256, i * 512 + part * 256 + 256)
+        c = c + lax.dot_general(
+            columns[:, i * 256 : i * 256 + 256], members[:, k], (((1,), (1,)), ((), ())), preferred_element_type=jnp.float32
+        )
+    return c
+
+
 def lane_sums(total):
     parts = [jnp.sum(total[s * 128 : (s + 1) * 128].T, axis=0, keepdims=True) for s in range(4)]
     return jnp.concatenate(parts, axis=1)
@@ -30,13 +40,13 @@
 
 def kernel(
     rounds, rows, out,
-    own, pieces_a, pieces_b, stage1, stage2, met1, met2, own_acc, acc1, acc2, row_acc, row_in, col_out, col_line, col_stage, col_plane,
+    own, pieces_a, pieces_b, stage1, stage2, met1_a, met1_b, scores, met2, own_acc, acc1, acc2, row_acc, row_in, col_out, col_line, col_stage, col_plane,
     partners, hop_a, low_a, hop_b, low_b, pick1, pick2, back,
     line_y, line_h, line_z, other, spread_send, spread_recv, send1, recv1, send2, recv2,
     load, table, own_send, own_recv, fwd_send, fwd_recv, row_send, row_recv, col_send, col_recv,
 ):
     blk, grp = lax.axis_index("blk"), lax.axis_index("grp")
-    pieces = (pieces_a, pieces_b)
+    pieces, met1s = (pieces_a, pieces_b), (met1_a, met1_b)
     y, xx, h = blk // 16, (blk // 4) % 4, blk % 4
     e, c = grp // 2, grp % 2
 
@@ -222,10 +232,9 @@
         def send(k, carry):
             ty, tx, th, to, row = place(k)
             stage1[part, k] = pieces[part][pick1[ty * 16 + tx * 4 + th]]
-            col = pl.multiple_of(my_col + part * 256, 256)
             remote(
                 stage1.at[part, k],
-                met1.at[pl.ds(row, 16), pl.ds(col, 256)],
+                met1s[part].at[pl.ds(row, 16), pl.ds(half, 256)],
                 send1.at[part],
                 recv1.at[part],
                 at(ty, tx, th, to),
@@ -238,7 +247,7 @@
 
         lax.fori_loop(0, count, group, 0)
         lax.fori_loop(1 + count * per, GROUPS, send, 0)
-        met1[pl.ds(home, 16), pl.ds(pl.multiple_of(my_col + part * 256, 256), 256)] = pieces[part][pick1[blk]]
+        met1s[part][pl.ds(home, 16), pl.ds(half, 256)] = pieces[part][pick1[blk]]
 
     drain(pieces_a.at[pl.ds(0, GROUPS - 1)], spread_recv.at[0])
     pl.semaphore_wait(other, 1)
@@ -296,9 +305,15 @@
     own_sums = lane_sums(own_acc[...])
 
     drain(stage1.at[0, pl.ds(0, GROUPS - 1)], recv1.at[0])
+    for t in range(8):
+        member, part = t // 2, slice((t % 2) * TILE, (t % 2 + 1) * TILE)
+        scores[t] = half_scores(met1_a[...], own[member, part, :], 0)
     drain(stage1.at[1, pl.ds(0, GROUPS - 1)], recv1.at[1])
-    for member in range(4):
-        meet(met1, acc1, None, member)
+    for t in range(8):
+        member, part = t // 2, slice((t % 2) * TILE, (t % 2 + 1) * TILE)
+        terms = jnp.exp2((scores[t] + half_scores(met1_b[...], own[member, part, :], 1)) * RATE - RATE)
+        acc1[...] += terms[:, :128] + terms[:, 128:]
+        row_acc[member, :, part] += jnp.sum(terms.reshape(ROWS // 8, 8, TILE), axis=0)
 
     publish(0, acc1)
     for i in range(1, 8):
@@ -379,7 +394,9 @@
             pltpu.VMEM((GROUPS, 16, 256), bf16),
             pltpu.VMEM((2, GROUPS, 16, 256), bf16),
             pltpu.VMEM((GROUPS, 16, 256), bf16),
-            pltpu.VMEM((ROWS, WIDTH), bf16),
+            pltpu.VMEM((ROWS, WIDTH // 2), bf16),
+            pltpu.VMEM((ROWS, WIDTH // 2), bf16),
+            pltpu.VMEM((8, ROWS, TILE), f32),
             pltpu.VMEM((ROWS, WIDTH), bf16),
             pltpu.VMEM((ROWS, 128), f32),
             pltpu.VMEM((ROWS, 128), f32),

time: 92.3 us -> 92.5 us (level)
  no operation moved by 1% of the time
where the time goes in v6:
time: 92.5 us; the launch traced here: 92.2 us
  Pallas kernels  90.9 us (98%)
  local copies, waits for them, and re-layouts  1.26 us (1%)
    pallas_call x1, Pallas kernels, body(): pl.pallas_call(kernel, out_shape=jax.ShapeDtypeStruct((4, 128), f32), in_...  90.9 us

profile of v6, /device:TPU:8, one launch (start us, length us, event | category | flops | bytes accessed | tf_op | source)
XLA Modules:
  0.0 92.2 jit_solution(5516474722014891963)
XLA Ops:
  0.0 90.9 %shard_map.28 = f32[4,128]{1,0:T(4,128)} custom-call(s32[3,64]{1,0:T(4,128)} %rounds.1, bf16[512,1024]{1,0:T(8,128)(2,1)} %rows.1), custom_call_target="tpu_custom_call" | custom-call | flops 6442450944 | bytes 1048576 | tf_op jit(solution)/shard_map/pallas_call | solution.py:383
  90.9 1.3 %copy.4 = f32[512]{0:T(512)} copy(f32[512]{0:T(512)} %bitcast.1) | data formatting | bytes 4096
